TPU v7x, 256 devices: a whole 4x4x8 slice. The times are simulated.
256 devices in a mesh: az: 32 (over x_lo, z, core), rad: 8 (over y, x_hi).
Axes of the slice: x: 4 (x_hi: 2, x_lo: 2; x = x_hi * 2 + x_lo), y: 4, z: 8, core: 2. Of those that a mesh axis runs over, the one named last changes fastest.
Arguments:
- state: float32 [8, 16, 256, 4096], P(None, None, 'rad', 'az'), may hold values from -6 to 6
- shift_counts: int32 [256], P('rad'), may hold values from 0 to 4095, as said below
- residual_speed: float32 [256], P('rad'), may hold values from -0.5 to 0.5
Outputs:
- evolved: float32 [8, 16, 256, 4096], P(None, None, 'rad', 'az')
Inputs may be any that keep to these rules, and one draw needn't show every extreme that they name: `shift_counts`: some row carries by 0 cells and some by 4096 - 1 cells in every draw.
All inputs are finite; a program needn't handle non-finite values.
Results may differ from a plain program's by a relative error of at most 0.00002.
Values sent between devices are 32-bit elements; how exact they have to be, the bound alone decides.
A program may use at most 128 MiB of HBM per device.

v0:
```python
import jax
import jax.numpy as jnp
from jax import lax
from jax.sharding import PartitionSpec as P

STEPS = 2


time_step = 0.2
viscosity = 0.1
shear_rate = 1.5


def shifted(value, axis, steps):
    count = lax.axis_size(axis)
    pairs = [(source, (source + steps) % count) for source in range(count)]
    return lax.ppermute(value, axis, pairs)


def extended(cells, sides, width, closed):
    for axis, dim in sides:
        count = lax.axis_size(axis)
        ends = count if closed else count - 1
        head = lax.slice_in_dim(cells, 0, width, axis=dim)
        tail = lax.slice_in_dim(cells, cells.shape[dim] - width, cells.shape[dim], axis=dim)
        cells = jnp.concatenate(
            [
                lax.ppermute(tail, axis, [(i, (i + 1) % count) for i in range(ends)]),
                cells,
                lax.ppermute(head, axis, [((i + 1) % count, i) for i in range(ends)]),
            ],
            axis=dim,
        )
    return cells


def window_rows(joined, starts, length):

    def one_row(row_block, start):
        return lax.dynamic_slice_in_dim(row_block, start, length, 2)

    return jax.vmap(one_row, in_axes=(2, 0), out_axes=2)(joined, starts)


def transport(fields, lower, upper, speed):
    weight = speed[None, None, :, None]
    forward = jnp.maximum(weight, 0.0)
    backward = jnp.minimum(weight, 0.0)
    return fields - forward * (fields - lower) - backward * (upper - fields)


def update(fields, padded, omega):
    north = padded[:, :, 2:]
    south = padded[:, :, :-2]
    radial_diff = (north - south) * 0.5
    radial_lap = north - 2.0 * fields + south
    upward = jnp.roll(fields, -1, 1)
    downward = jnp.roll(fields, 1, 1)
    vertical_diff = (upward - downward) * 0.5
    vertical_lap = upward - 2.0 * fields + downward
    spin = omega[None, :, None]
    rates = [
        -(radial_diff[1] + vertical_diff[3]),
        -radial_diff[0] + 2.0 * spin * fields[2] + vertical_diff[4],
        -(2.0 - shear_rate) * spin * fields[1] + vertical_diff[5],
        -vertical_diff[0],
        vertical_diff[1],
        vertical_diff[2] - shear_rate * spin * fields[4],
        -radial_diff[1],
        -(radial_diff[1] + vertical_diff[3]),
    ]
    return fields + viscosity * (radial_lap + vertical_lap) + time_step * jnp.stack(rates)


def shards(state, shift_counts, residual_speed):
    row_count = state.shape[2]
    cell_count = state.shape[3]
    az_devices = lax.axis_size("az")
    rad_devices = lax.axis_size("rad")
    radius = (lax.axis_index("rad") * row_count + jnp.arange(row_count, dtype=jnp.int32)).astype(
        jnp.float32
    )
    omega = (1.0 + radius / (row_count * rad_devices)) ** (-1.5)
    fields = state
    for step_index in range(STEPS):
        device_hops = shift_counts // cell_count
        remainder = shift_counts % cell_count
        for bit_index in range((az_devices - 1).bit_length()):
            moved = shifted(fields, "az", 1 << bit_index)
            chosen = (device_hops // (1 << bit_index) % 2 == 1)[None, None, :, None]
            fields = jnp.where(chosen, moved, fields)
        before = shifted(fields, "az", 1)
        joined = jnp.concatenate([before, fields], axis=3)
        fields = window_rows(joined, cell_count - remainder, cell_count)
        padded = extended(fields, (("az", 3),), 1, True)
        fields = transport(fields, padded[..., :-2], padded[..., 2:], residual_speed)
        padded = extended(fields, (("rad", 2),), 1, False)
        fields = update(fields, padded, omega)
    return fields


def solution(mesh):
    placed = (P(None, None, "rad", "az"), P("rad"), P("rad"))
    return jax.shard_map(
        shards, mesh=mesh, in_specs=placed, out_specs=P(None, None, "rad", "az"), check_vma=False
    )
```

profile of v0, /device:TPU:1, one launch (start us, length us, event | category | flops | bytes accessed | tf_op | source)
XLA Modules:
  0.0 888.6 jit_solution(1429393183815485728)
XLA Ops:
  0.0 3.0 collective-permute-start
  3.7 22.6 %collective-permute-done = f32[8,16,32,128]{3,2,1,0:T(8,128)S(1)} collective-permute-done((f32[8,16,32,128]{3,2,1,0:T(8,128)}, f32[8,16,32,128]{3,2,1,0:T(8,128)S(1)}, u32[]{:S(2)}, u32[]{:S(2)}) %collective-permute-start) | collective-permute-done | bytes 2097184 | tf_op jit(solution)/shard_map/ppermute | solution.py:17
  30.2 43.7 %collective-permute-done.1 = f32[8,16,32,128]{3,2,1,0:T(8,128)S(1)} collective-permute-done((f32[8,16,32,128]{3,2,1,0:T(8,128)S(1)}, f32[8,16,32,128]{3,2,1,0:T(8,128)S(1)}, u32[]{:S(2)}, u32[]{:S(2)}) %collective-permute-start.1) | collective-permute-done | bytes 2097184 | tf_op jit(solution)/shard_map/ppermute | solution.py:17
  74.4 5.9 collective-permute-start.2
  80.3 89.9 %collective-permute-done.2 = f32[8,16,32,128]{3,2,1,0:T(8,128)S(1)} collective-permute-done((f32[8,16,32,128]{3,2,1,0:T(8,128)S(1)}, f32[8,16,32,128]{3,2,1,0:T(8,128)S(1)}, u32[]{:S(2)}, u32[]{:S(2)}) %collective-permute-start.2) | collective-permute-done | bytes 2097184 | tf_op jit(solution)/shard_map/ppermute | solution.py:17
  170.8 51.5 %collective-permute-done.3 = f32[8,16,32,128]{3,2,1,0:T(8,128)S(1)} collective-permute-done((f32[8,16,32,128]{3,2,1,0:T(8,128)S(1)}, f32[8,16,32,128]{3,2,1,0:T(8,128)S(1)}, u32[]{:S(2)}, u32[]{:S(2)}) %collective-permute-start.3) | collective-permute-done | bytes 2097184 | tf_op jit(solution)/shard_map/ppermute | solution.py:17
  223.4 45.2 %collective-permute-done.4 = f32[8,16,32,128]{3,2,1,0:T(8,128)S(1)} collective-permute-done((f32[8,16,32,128]{3,2,1,0:T(8,128)S(1)}, f32[8,16,32,128]{3,2,1,0:T(8,128)S(1)}, u32[]{:S(2)}, u32[]{:S(2)}) %collective-permute-start.4) | collective-permute-done | bytes 2097184 | tf_op jit(solution)/shard_map/ppermute | solution.py:17
  269.1 94.1 %collective-permute-start.5 = (f32[8,16,32,128]{3,2,1,0:T(8,128)S(1)}, f32[8,16,32,128]{3,2,1,0:T(8,128)}, u32[]{:S(2)}, u32[]{:S(2)}) collective-permute-start(f32[8,16,32,128]{3,2,1,0:T(8,128)S(1)} %broadcast_select_fusion.9), channel_id=1, source_target_pairs={{0,8},{8,16},{16,24},{24,32},{32,40},{40,48},{48,56},{56,64},{64,7... | collective-permute-start | bytes 6291464 | tf_op jit(solution)/shard_map/ppermute | solution.py:17
  363.3 22.9 %collective-permute-done.5 = f32[8,16,32,128]{3,2,1,0:T(8,128)} collective-permute-done((f32[8,16,32,128]{3,2,1,0:T(8,128)S(1)}, f32[8,16,32,128]{3,2,1,0:T(8,128)}, u32[]{:S(2)}, u32[]{:S(2)}) %collective-permute-start.5) | collective-permute-done | bytes 2097184 | tf_op jit(solution)/shard_map/ppermute | solution.py:17
  386.2 4.1 maximum_bitcast_fusion
  390.3 26.6 %copy.185 = f32[32,8,16,256]{2,1,0,3:T(8,128)} copy(f32[32,8,16,256]{3,0,2,1:T(8,128)} %maximum_bitcast_fusion) | data formatting | bytes 8388608 | tf_op jit(solution)/shard_map/vmap()/transpose | solution.py:40
  416.8 13.3 %gather_fusion = f32[32,8,16,128]{2,1,3,0:T(8,128)} fusion(f32[32,8,16,256]{2,1,0,3:T(8,128)} %copy.185, s32[32]{0:T(128)S(1)} %fusion.40), kind=kCustom, calls=%fused_computation | custom fusion | bytes 4194816 | tf_op jit(solution)/shard_map/vmap()/gather | solution.py:40
  430.1 8.2 copy.186
  438.3 2.8 fusion.48
  443.6 2.6 collective-permute-start.6
  454.5 3.9 fusion.8
  460.4 5.7 collective-permute-start.9
  471.5 23.0 %collective-permute-done.10 = f32[8,16,32,128]{3,2,1,0:T(8,128)S(1)} collective-permute-done((f32[8,16,32,128]{3,2,1,0:T(8,128)S(1)}, f32[8,16,32,128]{3,2,1,0:T(8,128)S(1)}, u32[]{:S(2)}, u32[]{:S(2)}) %collective-permute-start.10) | collective-permute-done | bytes 2097184 | tf_op jit(solution)/shard_map/ppermute | solution.py:17
  495.1 47.3 %collective-permute-done.11 = f32[8,16,32,128]{3,2,1,0:T(8,128)S(1)} collective-permute-done((f32[8,16,32,128]{3,2,1,0:T(8,128)S(1)}, f32[8,16,32,128]{3,2,1,0:T(8,128)S(1)}, u32[]{:S(2)}, u32[]{:S(2)}) %collective-permute-start.11) | collective-permute-done | bytes 2097184 | tf_op jit(solution)/shard_map/ppermute | solution.py:17
  543.0 91.1 %collective-permute-done.12 = f32[8,16,32,128]{3,2,1,0:T(8,128)S(1)} collective-permute-done((f32[8,16,32,128]{3,2,1,0:T(8,128)S(1)}, f32[8,16,32,128]{3,2,1,0:T(8,128)S(1)}, u32[]{:S(2)}, u32[]{:S(2)}) %collective-permute-start.12) | collective-permute-done | bytes 2097184 | tf_op jit(solution)/shard_map/ppermute | solution.py:17
  636.4 95.2 %collective-permute-done.13 = f32[8,16,32,128]{3,2,1,0:T(8,128)S(1)} collective-permute-done((f32[8,16,32,128]{3,2,1,0:T(8,128)S(1)}, f32[8,16,32,128]{3,2,1,0:T(8,128)S(1)}, u32[]{:S(2)}, u32[]{:S(2)}) %collective-permute-start.13) | collective-permute-done | bytes 2097184 | tf_op jit(solution)/shard_map/ppermute | solution.py:17
  732.2 46.6 %collective-permute-done.14 = f32[8,16,32,128]{3,2,1,0:T(8,128)S(1)} collective-permute-done((f32[8,16,32,128]{3,2,1,0:T(8,128)S(1)}, f32[8,16,32,128]{3,2,1,0:T(8,128)S(1)}, u32[]{:S(2)}, u32[]{:S(2)}) %collective-permute-start.14) | collective-permute-done | bytes 2097184 | tf_op jit(solution)/shard_map/ppermute | solution.py:17
  779.6 23.0 %collective-permute-done.15 = f32[8,16,32,128]{3,2,1,0:T(8,128)S(1)} collective-permute-done((f32[8,16,32,128]{3,2,1,0:T(8,128)S(1)}, f32[8,16,32,128]{3,2,1,0:T(8,128)S(1)}, u32[]{:S(2)}, u32[]{:S(2)}) %collective-permute-start.15) | collective-permute-done | bytes 2097184 | tf_op jit(solution)/shard_map/ppermute | solution.py:17
  805.1 26.6 %copy.191 = f32[32,8,16,256]{2,1,0,3:T(8,128)} copy(f32[32,8,16,256]{3,0,2,1:T(8,128)} %maximum_bitcast_fusion.1) | data formatting | bytes 8388608 | tf_op jit(solution)/shard_map/vmap()/transpose | solution.py:40
  831.7 13.3 %gather_fusion.1 = f32[32,8,16,128]{2,1,3,0:T(8,128)} fusion(f32[32,8,16,256]{2,1,0,3:T(8,128)} %copy.191, s32[32]{0:T(128)S(1)} %fusion.40), kind=kCustom, calls=%fused_computation.1 | custom fusion | bytes 4194816 | tf_op jit(solution)/shard_map/vmap()/gather | solution.py:40
  845.0 8.2 copy.192
  853.2 2.8 fusion.44
  858.4 2.5 collective-permute-start.16
  863.4 3.6 collective-permute-start.17
  871.3 3.9 fusion.2
  877.1 6.2 collective-permute-start.19
  885.8 2.6 multiply_add_fusion
  (76 shorter events, 45.9 us)
Async XLA Ops:
  0.0 26.3 %collective-permute-start = (f32[8,16,32,128]{3,2,1,0:T(8,128)}, f32[8,16,32,128]{3,2,1,0:T(8,128)S(1)}, u32[]{:S(2)}, u32[]{:S(2)}) collective-permute-start(f32[8,16,32,128]{3,2,1,0:T(8,128)} %param.3), channel_id=1, source_target_pairs={{0,8},{8,16},{16,24},{24,32},{32,40},{40,48},{48,56},{56,64},{64,7... | collective-permute-start | bytes 6291464 | tf_op jit(solution)/shard_map/ppermute | solution.py:17
  28.4 45.5 %collective-permute-start.1 = (f32[8,16,32,128]{3,2,1,0:T(8,128)S(1)}, f32[8,16,32,128]{3,2,1,0:T(8,128)S(1)}, u32[]{:S(2)}, u32[]{:S(2)}) collective-permute-start(f32[8,16,32,128]{3,2,1,0:T(8,128)S(1)} %broadcast_select_fusion.1), channel_id=1, source_target_pairs={{0,16},{8,24},{16,32},{24,40},{32,48},{40,56},{48,64},{56,72},{64,... | collective-permute-start | bytes 6291464 | tf_op jit(solution)/shard_map/ppermute | solution.py:17
  74.4 95.8 %collective-permute-start.2 = (f32[8,16,32,128]{3,2,1,0:T(8,128)S(1)}, f32[8,16,32,128]{3,2,1,0:T(8,128)S(1)}, u32[]{:S(2)}, u32[]{:S(2)}) collective-permute-start(f32[8,16,32,128]{3,2,1,0:T(8,128)S(1)} %broadcast_select_fusion.3), channel_id=1, source_target_pairs={{0,32},{8,40},{16,48},{24,56},{32,64},{40,72},{48,80},{56,88},{64,... | collective-permute-start | bytes 6291464 | tf_op jit(solution)/shard_map/ppermute | solution.py:17
  170.7 51.6 %collective-permute-start.3 = (f32[8,16,32,128]{3,2,1,0:T(8,128)S(1)}, f32[8,16,32,128]{3,2,1,0:T(8,128)S(1)}, u32[]{:S(2)}, u32[]{:S(2)}) collective-permute-start(f32[8,16,32,128]{3,2,1,0:T(8,128)S(1)} %broadcast_select_fusion.5), channel_id=1, source_target_pairs={{0,64},{8,72},{16,80},{24,88},{32,96},{40,104},{48,112},{56,120},{... | collective-permute-start | bytes 6291464 | tf_op jit(solution)/shard_map/ppermute | solution.py:17
  222.9 45.7 %collective-permute-start.4 = (f32[8,16,32,128]{3,2,1,0:T(8,128)S(1)}, f32[8,16,32,128]{3,2,1,0:T(8,128)S(1)}, u32[]{:S(2)}, u32[]{:S(2)}) collective-permute-start(f32[8,16,32,128]{3,2,1,0:T(8,128)S(1)} %broadcast_select_fusion.7), channel_id=1, source_target_pairs={{0,128},{8,136},{16,144},{24,152},{32,160},{40,168},{48,176},{56,1... | collective-permute-start | bytes 6291464 | tf_op jit(solution)/shard_map/ppermute | solution.py:17
  268.6 94.6 %copy-start = (s32[32]{0:T(128)S(1)}, s32[32]{0:T(128)}, u32[]{:S(2)}) copy-start(s32[32]{0:T(128)} %param.4) | copy-start | bytes 388
  268.6 94.7 %copy-start.1 = (f32[32]{0:T(128)S(1)}, f32[32]{0:T(128)}, u32[]{:S(2)}) copy-start(f32[32]{0:T(128)} %param.5) | copy-start | bytes 388
  269.1 117.1 %collective-permute-start.5 = (f32[8,16,32,128]{3,2,1,0:T(8,128)S(1)}, f32[8,16,32,128]{3,2,1,0:T(8,128)}, u32[]{:S(2)}, u32[]{:S(2)}) collective-permute-start(f32[8,16,32,128]{3,2,1,0:T(8,128)S(1)} %broadcast_select_fusion.9), channel_id=1, source_target_pairs={{0,8},{8,16},{16,24},{24,32},{32,40},{40,48},{48,56},{56,64},{64,7... | collective-permute-start | bytes 6291464 | tf_op jit(solution)/shard_map/ppermute | solution.py:17
  443.6 5.1 collective-permute-start.6
  448.6 3.8 collective-permute-start.7
  459.1 7.5 collective-permute-start.8
  460.4 6.8 collective-permute-start.9
  470.0 24.5 %collective-permute-start.10 = (f32[8,16,32,128]{3,2,1,0:T(8,128)S(1)}, f32[8,16,32,128]{3,2,1,0:T(8,128)S(1)}, u32[]{:S(2)}, u32[]{:S(2)}) collective-permute-start(f32[8,16,32,128]{3,2,1,0:T(8,128)S(1)} %multiply_add_fusion.1), channel_id=1, source_target_pairs={{0,8},{8,16},{16,24},{24,32},{32,40},{40,48},{48,56},{56,64},{64,7... | collective-permute-start | bytes 6291464 | tf_op jit(solution)/shard_map/ppermute | solution.py:17
  495.0 47.4 %collective-permute-start.11 = (f32[8,16,32,128]{3,2,1,0:T(8,128)S(1)}, f32[8,16,32,128]{3,2,1,0:T(8,128)S(1)}, u32[]{:S(2)}, u32[]{:S(2)}) collective-permute-start(f32[8,16,32,128]{3,2,1,0:T(8,128)S(1)} %broadcast_select_fusion), channel_id=1, source_target_pairs={{0,16},{8,24},{16,32},{24,40},{32,48},{40,56},{48,64},{56,72},{64,... | collective-permute-start | bytes 6291464 | tf_op jit(solution)/shard_map/ppermute | solution.py:17
  542.9 91.2 %collective-permute-start.12 = (f32[8,16,32,128]{3,2,1,0:T(8,128)S(1)}, f32[8,16,32,128]{3,2,1,0:T(8,128)S(1)}, u32[]{:S(2)}, u32[]{:S(2)}) collective-permute-start(f32[8,16,32,128]{3,2,1,0:T(8,128)S(1)} %broadcast_select_fusion.2), channel_id=1, source_target_pairs={{0,32},{8,40},{16,48},{24,56},{32,64},{40,72},{48,80},{56,88},{64,... | collective-permute-start | bytes 6291464 | tf_op jit(solution)/shard_map/ppermute | solution.py:17
  634.7 96.8 %collective-permute-start.13 = (f32[8,16,32,128]{3,2,1,0:T(8,128)S(1)}, f32[8,16,32,128]{3,2,1,0:T(8,128)S(1)}, u32[]{:S(2)}, u32[]{:S(2)}) collective-permute-start(f32[8,16,32,128]{3,2,1,0:T(8,128)S(1)} %broadcast_select_fusion.4), channel_id=1, source_target_pairs={{0,64},{8,72},{16,80},{24,88},{32,96},{40,104},{48,112},{56,120},{... | collective-permute-start | bytes 6291464 | tf_op jit(solution)/shard_map/ppermute | solution.py:17
  732.1 46.7 %collective-permute-start.14 = (f32[8,16,32,128]{3,2,1,0:T(8,128)S(1)}, f32[8,16,32,128]{3,2,1,0:T(8,128)S(1)}, u32[]{:S(2)}, u32[]{:S(2)}) collective-permute-start(f32[8,16,32,128]{3,2,1,0:T(8,128)S(1)} %broadcast_select_fusion.6), channel_id=1, source_target_pairs={{0,128},{8,136},{16,144},{24,152},{32,160},{40,168},{48,176},{56,1... | collective-permute-start | bytes 6291464 | tf_op jit(solution)/shard_map/ppermute | solution.py:17
  779.3 23.3 %collective-permute-start.15 = (f32[8,16,32,128]{3,2,1,0:T(8,128)S(1)}, f32[8,16,32,128]{3,2,1,0:T(8,128)S(1)}, u32[]{:S(2)}, u32[]{:S(2)}) collective-permute-start(f32[8,16,32,128]{3,2,1,0:T(8,128)S(1)} %broadcast_select_fusion.8), channel_id=1, source_target_pairs={{0,8},{8,16},{16,24},{24,32},{32,40},{40,48},{48,56},{56,64},{64,7... | collective-permute-start | bytes 6291464 | tf_op jit(solution)/shard_map/ppermute | solution.py:17
  858.4 8.5 collective-permute-start.16
  863.4 5.8 collective-permute-start.17
  875.8 8.0 collective-permute-start.18
  877.1 7.5 collective-permute-start.19
where the time goes:
time: 902 us; the launch traced here: 889 us
  waiting for transfers between devices  605 us (67%)
  starting transfers between devices  132 us (15%)
  local copies, waits for them, and re-layouts  121 us (13%)
  other arithmetic  29.5 us (3%)
    ppermute x12, waiting for transfers between devices, shifted(): return lax.ppermute(value, axis, pairs)  602 us
    ppermute x12, starting transfers between devices, shifted(): return lax.ppermute(value, axis, pairs)  109 us
    transpose x2, local copies, waits for them, and re-layouts, one_row(): return lax.dynamic_slice_in_dim(row_block, start, length, 2)  53.1 us
    gather x4, local copies, waits for them, and re-layouts, one_row(): return lax.dynamic_slice_in_dim(row_block, start, length, 2)  43 us
  transfers between devices with their start and end apart: 20, of which 15 were waited for; matrix products, arithmetic and copies ran while one was open for 1% of the time, Pallas kernels for 0%

commit v1 on v0

v1 whole, which is shorter than its diff:
```python
import jax
import jax.numpy as jnp
from jax import lax
from jax.experimental import pallas as pl
from jax.experimental.pallas import tpu as pltpu
from jax.sharding import PartitionSpec as P

FIELDS, NZ, ROWS, LANES = 8, 16, 32, 128
AZ, RAD = 32, 8
Z_CHIPS = 8
PART = 4
ORDER = (0, 3, 1, 2)

time_step = 0.2
viscosity = 0.1
shear_rate = 1.5

MESH = pl.DeviceIdType.MESH


def place(index, rad):
    core = lax.rem(index, 2)
    z = lax.rem(index // 2, Z_CHIPS)
    x = index // (2 * Z_CHIPS)
    block = z + lax.rem(rad, 2) * (Z_CHIPS - 1 - 2 * z)
    quarter = 2 * x + lax.rem(core + x, 2)
    return block, quarter


def owner(block, quarter, rad):
    z = block + lax.rem(rad, 2) * (Z_CHIPS - 1 - 2 * block)
    x = quarter // 2
    core = lax.rem(lax.rem(quarter, 2) + x, 2)
    return (x * Z_CHIPS + z) * 2 + core


def field_vector(values):
    row = lax.broadcasted_iota(jnp.int32, (FIELDS, LANES), 0)
    first = values[0]
    result = jnp.full((FIELDS, LANES), first, jnp.asarray(first).dtype)
    for index in range(1, FIELDS):
        result = jnp.where(row == index, values[index], result)
    return result


def picked(value, source):
    count = value.shape[0]
    flat = value.reshape(count * FIELDS, LANES)
    parts = [
        jnp.take_along_axis(flat[i * FIELDS : (i + 1) * FIELDS], source, axis=0)
        for i in range(count)
    ]
    return jnp.stack(parts)


def evolve(v, north, south, up, down, spin):
    from_radial = field_vector([1, 0, 2, 3, 4, 5, 1, 1])
    from_vertical = field_vector([3, 4, 5, 0, 1, 2, 6, 3])
    from_spin = field_vector([0, 2, 1, 3, 4, 4, 6, 7])
    half = 0.5 * time_step
    radial_factor = field_vector([-half, -half, 0.0, 0.0, 0.0, 0.0, -half, -half])
    vertical_factor = field_vector([-half, half, half, -half, half, half, 0.0, -half])
    spin_factor = field_vector(
        [
            0.0,
            2.0 * time_step,
            -(2.0 - shear_rate) * time_step,
            0.0,
            0.0,
            -shear_rate * time_step,
            0.0,
            0.0,
        ]
    )
    laplacian = (north + south) + (up + down) - 4.0 * v
    rates = (
        radial_factor * picked(north - south, from_radial)
        + vertical_factor * picked(up - down, from_vertical)
        + (spin_factor * spin) * picked(v, from_spin)
    )
    return v + viscosity * laplacian + rates


def transport(source, target, speed):
    forward = jnp.maximum(speed, 0.0)
    backward = jnp.minimum(speed, 0.0)

    def body(k, carry):
        shape = (PART * FIELDS, LANES)
        lane = lax.broadcasted_iota(jnp.int32, shape, 1)
        here = source[k].reshape(shape)
        before = source[lax.rem(k + AZ - 1, AZ)].reshape(shape)
        after = source[lax.rem(k + 1, AZ)].reshape(shape)
        lower = pltpu.roll(jnp.where(lane == LANES - 1, before, here), 1, 1)
        upper = pltpu.roll(jnp.where(lane == 0, after, here), LANES - 1, 1)
        moved = here - forward * (here - lower) - backward * (upper - here)
        target[k] = moved.reshape(PART, FIELDS, LANES)
        return carry

    lax.fori_loop(0, AZ, body, 0, unroll=2)


def rotate(source, target, count):
    hops = count // LANES
    lanes = lax.rem(count, LANES)

    def body(k, carry):
        shape = (PART * FIELDS, LANES)
        lane = lax.broadcasted_iota(jnp.int32, shape, 1)
        here = source[lax.rem(k - hops + AZ, AZ)].reshape(shape)
        before = source[lax.rem(k - hops + 2 * AZ - 1, AZ)].reshape(shape)
        joined = jnp.where(lane >= LANES - lanes, before, here)
        target[k] = pltpu.roll(joined, lanes, 1).reshape(PART, FIELDS, LANES)
        return carry

    lax.fori_loop(0, AZ, body, 0, unroll=2)


def kernel(
    state, counts, speeds, spins, out,
    packed, wide, moved, evolved, *scratch,
):
    received = scratch[0:4]
    carried = scratch[4:8]
    ready = scratch[8:12]
    cell_below = scratch[12:16]
    cell_above = scratch[16:20]
    row_south, row_north = scratch[20:22]
    (in_send, in_recv, out_send, out_recv, own, up_send, up_recv, down_send, down_recv,
     row_send, row_recv, edge_send, edge_recv) = scratch[22:]

    me = lax.axis_index("az")
    rad = lax.axis_index("rad")
    rad_next = lax.rem(rad + 1, RAD)
    rad_last = lax.rem(rad + RAD - 1, RAD)
    block, quarter = place(me, rad)

    barrier = pltpu.get_barrier_semaphore()

    def greet(k, carry):
        pl.semaphore_signal(
            barrier, inc=1, device_id={"az": lax.rem(me + k, AZ)}, device_id_type=MESH
        )
        return carry

    lax.fori_loop(1, AZ, greet, 0)
    for other in (rad_next, rad_last):
        pl.semaphore_signal(barrier, inc=1, device_id={"rad": other}, device_id_type=MESH)

    def pack(row, carry):
        for cell in range(NZ):
            packed[row, cell] = state[pl.ds(cell * ROWS + row, FIELDS, stride=NZ * ROWS), :]
        return carry

    lax.fori_loop(0, ROWS, pack, 0)
    pl.semaphore_wait(barrier, AZ + 1)

    def send_in(c):
        own_copy = pltpu.make_async_copy(
            packed.at[PART * block + c, pl.ds(PART * quarter, PART)], received[c].at[me], own.at[c]
        )
        own_copy.start()

        def body(k, carry):
            to = lax.rem(me + k, AZ)
            to_block, to_quarter = place(to, rad)
            pltpu.make_async_remote_copy(
                src_ref=packed.at[PART * to_block + c, pl.ds(PART * to_quarter, PART)],
                dst_ref=received[c].at[me],
                send_sem=in_send.at[c],
                recv_sem=in_recv.at[c],
                device_id={"az": to},
                device_id_type=MESH,
            ).start()
            return carry

        lax.fori_loop(1, AZ, body, 0)
        return own_copy

    def send_out(c):
        own_copy = pltpu.make_async_copy(
            ready[c].at[me], wide.at[1 + PART * block + c, pl.ds(PART * quarter, PART)],
            own.at[PART + c],
        )
        own_copy.start()

        def body(k, carry):
            to = lax.rem(me + k, AZ)
            pltpu.make_async_remote_copy(
                src_ref=ready[c].at[to],
                dst_ref=wide.at[1 + PART * block + c, pl.ds(PART * quarter, PART)],
                send_sem=out_send.at[c],
                recv_sem=out_recv.at[c],
                device_id={"az": to},
                device_id_type=MESH,
            ).start()
            return carry

        lax.fori_loop(1, AZ, body, 0)
        return own_copy

    def whole(buffer, send_sem, recv_sem):
        part = buffer.at[pl.ds(0, AZ - 1)]
        return pltpu.make_async_remote_copy(
            src_ref=part, dst_ref=part, send_sem=send_sem, recv_sem=recv_sem,
            device_id={"az": lax.rem(me + 1, AZ)}, device_id_type=MESH,
        )

    def cells(c):
        to_down = owner(block, lax.rem(quarter + 3, 4), rad)
        to_up = owner(block, lax.rem(quarter + 1, 4), rad)
        down = pltpu.make_async_remote_copy(
            src_ref=carried[c].at[:, 0], dst_ref=cell_above[c],
            send_sem=down_send.at[c], recv_sem=down_recv.at[c],
            device_id={"az": to_down}, device_id_type=MESH,
        )
        up = pltpu.make_async_remote_copy(
            src_ref=carried[c].at[:, PART - 1], dst_ref=cell_below[c],
            send_sem=up_send.at[c], recv_sem=up_recv.at[c],
            device_id={"az": to_up}, device_id_type=MESH,
        )
        down.start()
        up.start()
        return down, up

    def row_copy(which, source, target, step):
        other = block + step
        to_rad = lax.rem(rad + (other + Z_CHIPS) // Z_CHIPS - 1 + RAD, RAD)
        to_block = lax.rem(other + Z_CHIPS, Z_CHIPS)
        copy = pltpu.make_async_remote_copy(
            src_ref=source, dst_ref=target,
            send_sem=row_send.at[which], recv_sem=row_recv.at[which],
            device_id={"az": owner(to_block, quarter, to_rad), "rad": to_rad},
            device_id_type=MESH,
        )
        copy.start()
        return copy

    def first_step(c):
        row = PART * block + c
        transport(received[c], moved, speeds[row])
        rotate(moved, carried[c], counts[row])

    has_south = jnp.logical_or(rad > 0, block > 0)
    has_north = jnp.logical_or(rad < RAD - 1, block < Z_CHIPS - 1)

    def second_step(c):
        row = PART * block + c
        spin = spins[row]

        def body(k, carry):
            v = carried[c][k]
            if c > 0:
                south = carried[c - 1][k]
            else:
                south = row_south[k]
                south = jnp.where(has_south, south, jnp.zeros_like(south))
            if c < PART - 1:
                north = carried[c + 1][k]
            else:
                north = row_north[k]
                north = jnp.where(has_north, north, jnp.zeros_like(north))
            up = jnp.concatenate([v[1:], cell_above[c][k][None]], axis=0)
            down = jnp.concatenate([cell_below[c][k][None], v[:-1]], axis=0)
            evolved[k] = evolve(v, north, south, up, down, spin)
            return carry

        lax.fori_loop(0, AZ, body, 0)
        transport(evolved, moved, speeds[row])
        rotate(moved, ready[c], counts[row])

    ins, outs, halos = {}, {}, {}

    def wait_in(c):
        ins[c].wait()
        whole(received[c], in_send.at[c], in_recv.at[c]).wait_recv()

    def wait_cells(c):
        for copy in halos[c]:
            copy.wait_recv()

    def wait_out(c):
        outs[c].wait()
        whole(ready[c], out_send.at[c], out_recv.at[c]).wait_recv()

    ins[0] = send_in(0)
    ins[3] = send_in(3)

    wait_in(0)
    ins[1] = send_in(1)
    first_step(0)
    to_last = row_copy(0, carried[0], row_north, -1)
    halos[0] = cells(0)

    wait_in(3)
    ins[2] = send_in(2)
    first_step(3)
    to_next = row_copy(1, carried[3], row_south, 1)
    halos[3] = cells(3)

    wait_in(1)
    first_step(1)
    halos[1] = cells(1)

    to_next.wait_recv()
    wait_cells(0)
    second_step(0)
    outs[0] = send_out(0)

    wait_in(2)
    first_step(2)
    halos[2] = cells(2)

    to_last.wait_recv()
    wait_cells(3)
    second_step(3)
    outs[3] = send_out(3)
    for c in (1, 2):
        wait_cells(c)
        second_step(c)
        outs[c] = send_out(c)

    def edge(which, source, target, to):
        copy = pltpu.make_async_remote_copy(
            src_ref=wide.at[source], dst_ref=wide.at[target],
            send_sem=edge_send.at[which], recv_sem=edge_recv.at[which],
            device_id={"rad": to}, device_id_type=MESH,
        )
        copy.start()
        return copy

    wait_out(0)
    edge_last = edge(0, 1, ROWS + 1, rad_last)
    wait_out(3)
    edge_next = edge(1, ROWS, 0, rad_next)
    wait_out(1)
    wait_out(2)
    edge_last.wait()
    edge_next.wait()

    @pl.when(rad == 0)
    def _():
        wide[0] = jnp.zeros((NZ, FIELDS, LANES), jnp.float32)

    @pl.when(rad == RAD - 1)
    def _():
        wide[ROWS + 1] = jnp.zeros((NZ, FIELDS, LANES), jnp.float32)

    def last(row, carry):
        spin = spins[row]
        for cell in range(NZ):
            pick = lambda r, c: wide[r, c][None]
            result = evolve(
                pick(row + 1, cell), pick(row + 2, cell), pick(row, cell),
                pick(row + 1, (cell + 1) % NZ), pick(row + 1, (cell + NZ - 1) % NZ), spin,
            )
            out[pl.ds(cell * ROWS + row, FIELDS, stride=NZ * ROWS), :] = result[0]
        return carry

    lax.fori_loop(0, ROWS, last, 0)

    for c in ORDER:
        whole(received[c], in_send.at[c], in_recv.at[c]).wait_send()
        whole(ready[c], out_send.at[c], out_recv.at[c]).wait_send()
        for copy in halos[c]:
            copy.wait_send()
    to_last.wait_send()
    to_next.wait_send()


def shards(state, shift_counts, residual_speed):
    radius = (lax.axis_index("rad") * ROWS + jnp.arange(ROWS, dtype=jnp.int32)).astype(jnp.float32)
    omega = (1.0 + radius / (ROWS * RAD)) ** (-1.5)
    circle = (AZ, PART, FIELDS, LANES)
    vmem = pl.BlockSpec(memory_space=pltpu.VMEM)
    smem = pl.BlockSpec(memory_space=pltpu.SMEM)
    f32 = jnp.float32
    dma = pltpu.SemaphoreType.DMA
    result = pl.pallas_call(
        kernel,
        out_shape=jax.ShapeDtypeStruct((FIELDS * NZ * ROWS, LANES), f32),
        in_specs=[vmem, smem, smem, smem],
        out_specs=vmem,
        scratch_shapes=[
            pltpu.VMEM((ROWS, NZ, FIELDS, LANES), f32),
            pltpu.VMEM((ROWS + 2, NZ, FIELDS, LANES), f32),
            pltpu.VMEM(circle, f32),
            pltpu.VMEM(circle, f32),
        ]
        + [pltpu.VMEM(circle, f32)] * 12
        + [pltpu.VMEM((AZ, FIELDS, LANES), f32)] * 8
        + [pltpu.VMEM(circle, f32)] * 2
        + [dma((4,)), dma((4,)), dma((4,)), dma((4,)), dma((8,))]
        + [dma((4,)), dma((4,)), dma((4,)), dma((4,))]
        + [dma((2,)), dma((2,)), dma((2,)), dma((2,))],
        compiler_params=pltpu.CompilerParams(
            collective_id=0, has_side_effects=True, vmem_limit_bytes=48 << 20
        ),
    )(state.reshape(FIELDS * NZ * ROWS, LANES), shift_counts, residual_speed, omega)
    return result.reshape(FIELDS, NZ, ROWS, LANES)


def solution(mesh):
    placed = (P(None, None, "rad", "az"), P("rad"), P("rad"))
    return jax.shard_map(
        shards, mesh=mesh, in_specs=placed, out_specs=P(None, None, "rad", "az"), check_vma=False
    )
```

time: 902 us -> 128 us (0.14); the launches traced: 889 us -> 128 us
  waiting for transfers between devices: 605 us -> 0 us
  starting transfers between devices: 132 us -> 0 us
  Pallas kernels: 0 us -> 123 us
  local copies, waits for them, and re-layouts: 121 us -> 4.22 us
  other arithmetic: 29.5 us -> 0.01 us
    ppermute x20 -> x0, waiting for transfers between devices: 605 us -> none  [the longest x12 602 us: shifted(): return lax.ppermute(value, axis, pairs)]
    ppermute x20 -> x0, starting transfers between devices: 132 us -> none  [the longest x12 109 us: shifted(): return lax.ppermute(value, axis, pairs)]
    pallas_call x0 -> x1, Pallas kernels: none -> 123 us  [shards(): pl.pallas_call(kernel, out_shape=jax.ShapeDtypeStruct((FIELDS * NZ * ROWS...]
    transpose x2 -> x0, local copies, waits for them, and re-layouts: 53.1 us -> none  [one_row(): return lax.dynamic_slice_in_dim(row_block, start, length, 2)]
    gather x4 -> x0, local copies, waits for them, and re-layouts: 43 us -> none  [one_row(): return lax.dynamic_slice_in_dim(row_block, start, length, 2)]
    slice x12 -> x0, local copies, waits for them, and re-layouts: 16.5 us -> none  [the longest x6 10.7 us: extended(): lax.slice_in_dim(cells, cells.shape[dim] - width, cells.shape[dim], axis=...]
  transfers between devices with their start and end apart: 20 -> 0, of which waited for: 15 -> 0; matrix products, arithmetic and copies ran while one was open for 1% -> 0% of each run, Pallas kernels for 0% -> 0%
where the time goes in v1:
time: 128 us
  Pallas kernels  123 us (96%)
  local copies, waits for them, and re-layouts  4.22 us (3%)
    pallas_call x1, Pallas kernels, shards(): pl.pallas_call(kernel, out_shape=jax.ShapeDtypeStruct((FIELDS * NZ * ROWS...  123 us
    unnamed x7, local copies, waits for them, and re-layouts  4.22 us

profile of v1, /device:TPU:1, one launch (start us, length us, event | category | flops | bytes accessed | tf_op | source)
XLA Modules:
  0.0 127.6 jit_solution(16017996932051268228)
XLA Ops:
  0.0 0.0 copy-start
  0.0 1.6 %copy-done = f32[8,16,32,128]{3,2,1,0:T(8,128)S(1)} copy-done((f32[8,16,32,128]{3,2,1,0:T(8,128)S(1)}, f32[8,16,32,128]{3,2,1,0:T(8,128)}, u32[]{:S(2)}) %copy-start) | copy-done | bytes 2097176
  1.6 0.0 copy-start.1
  1.6 0.7 copy-done.1
  2.3 0.0 copy-start.2
  2.3 0.7 copy-done.2
  2.9 123.4 %shard_map.37 = f32[4096,128]{1,0:T(8,128)S(1)} custom-call(f32[4096,128]{1,0:T(8,128)S(1)} %bitcast.3, s32[32]{0:T(128)S(1)} %copy-done.1, f32[32]{0:T(128)S(1)} %copy-done.2, f32[32]{0:T(128)S(1)} %add_power_fusion.spins), custom_call_target="tpu_custom_call" | custom-call | tf_op jit(solution)/shard_map/pallas_call | solution.py:379
  126.3 1.3 %copy.5 = f32[8,16,32,128]{3,2,1,0:T(8,128)} copy(f32[8,16,32,128]{3,2,1,0:T(8,128)S(1)} %bitcast.2) | data formatting | bytes 4194304
  (1 shorter events, 0.0 us)
Async XLA Ops:
  0.0 1.6 %copy-start = (f32[8,16,32,128]{3,2,1,0:T(8,128)S(1)}, f32[8,16,32,128]{3,2,1,0:T(8,128)}, u32[]{:S(2)}) copy-start(f32[8,16,32,128]{3,2,1,0:T(8,128)} %param.3) | copy-start | bytes 6291460
  1.6 0.7 copy-start.1
  2.3 0.7 copy-start.2

commit v2 on v1

--- a/solution.py
+++ b/solution.py
@@ -53,72 +53,76 @@
     return jnp.stack(parts)
 
 
-def evolve(v, north, south, up, down, spin):
-    from_radial = field_vector([1, 0, 2, 3, 4, 5, 1, 1])
-    from_vertical = field_vector([3, 4, 5, 0, 1, 2, 6, 3])
-    from_spin = field_vector([0, 2, 1, 3, 4, 4, 6, 7])
+def field_tables():
     half = 0.5 * time_step
-    radial_factor = field_vector([-half, -half, 0.0, 0.0, 0.0, 0.0, -half, -half])
-    vertical_factor = field_vector([-half, half, half, -half, half, half, 0.0, -half])
-    spin_factor = field_vector(
-        [
-            0.0,
-            2.0 * time_step,
-            -(2.0 - shear_rate) * time_step,
-            0.0,
-            0.0,
-            -shear_rate * time_step,
-            0.0,
-            0.0,
-        ]
+    return (
+        field_vector([1, 0, 2, 3, 4, 5, 1, 1]),
+        field_vector([3, 4, 5, 0, 1, 2, 6, 3]),
+        field_vector([0, 2, 1, 3, 4, 4, 6, 7]),
+        field_vector([-half, -half, 0.0, 0.0, 0.0, 0.0, -half, -half]),
+        field_vector([-half, half, half, -half, half, half, 0.0, -half]),
+        field_vector(
+            [
+                0.0,
+                2.0 * time_step,
+                -(2.0 - shear_rate) * time_step,
+                0.0,
+                0.0,
+                -shear_rate * time_step,
+                0.0,
+                0.0,
+            ]
+        ),
     )
+
+
+def spin_of(row, rad, spin_factor):
+    radius = jnp.full((FIELDS, LANES), rad * ROWS + row, jnp.int32).astype(jnp.float32)
+    distance = 1.0 + radius / (ROWS * RAD)
+    return spin_factor / (distance * jnp.sqrt(distance))
+
+
+def evolve(v, north, south, up, down, tables, spin):
+    from_radial, from_vertical, from_spin, radial_factor, vertical_factor, _ = tables
     laplacian = (north + south) + (up + down) - 4.0 * v
     rates = (
         radial_factor * picked(north - south, from_radial)
         + vertical_factor * picked(up - down, from_vertical)
-        + (spin_factor * spin) * picked(v, from_spin)
+        + spin * picked(v, from_spin)
     )
     return v + viscosity * laplacian + rates
 
 
-def transport(source, target, speed):
+def carry(source, target, speed, count):
+    shape = (PART * FIELDS, LANES)
     forward = jnp.maximum(speed, 0.0)
     backward = jnp.minimum(speed, 0.0)
-
-    def body(k, carry):
-        shape = (PART * FIELDS, LANES)
-        lane = lax.broadcasted_iota(jnp.int32, shape, 1)
-        here = source[k].reshape(shape)
-        before = source[lax.rem(k + AZ - 1, AZ)].reshape(shape)
-        after = source[lax.rem(k + 1, AZ)].reshape(shape)
-        lower = pltpu.roll(jnp.where(lane == LANES - 1, before, here), 1, 1)
-        upper = pltpu.roll(jnp.where(lane == 0, after, here), LANES - 1, 1)
-        moved = here - forward * (here - lower) - backward * (upper - here)
-        target[k] = moved.reshape(PART, FIELDS, LANES)
-        return carry
-
-    lax.fori_loop(0, AZ, body, 0, unroll=2)
-
-
-def rotate(source, target, count):
     hops = count // LANES
     lanes = lax.rem(count, LANES)
-
-    def body(k, carry):
-        shape = (PART * FIELDS, LANES)
-        lane = lax.broadcasted_iota(jnp.int32, shape, 1)
+    lane = lax.broadcasted_iota(jnp.int32, shape, 1)
+    own_mask = lane >= LANES - lanes
+    low_mask = lane >= LANES - 1 - lanes
+    high_mask = lane >= LANES + 1 - lanes
+    next_mask = lane + lanes == 0
+
+    def body(k, nothing):
         here = source[lax.rem(k - hops + AZ, AZ)].reshape(shape)
         before = source[lax.rem(k - hops + 2 * AZ - 1, AZ)].reshape(shape)
-        joined = jnp.where(lane >= LANES - lanes, before, here)
-        target[k] = pltpu.roll(joined, lanes, 1).reshape(PART, FIELDS, LANES)
-        return carry
-
-    lax.fori_loop(0, AZ, body, 0, unroll=2)
+        after = source[lax.rem(k - hops + AZ + 1, AZ)].reshape(shape)
+        cells = jnp.where(own_mask, before, here)
+        lower = pltpu.roll(jnp.where(low_mask, before, here), 1, 1)
+        upper = jnp.where(next_mask, after, jnp.where(high_mask, before, here))
+        upper = pltpu.roll(upper, LANES - 1, 1)
+        moved = cells - forward * (cells - lower) - backward * (upper - cells)
+        target[k] = pltpu.roll(moved, lanes, 1).reshape(PART, FIELDS, LANES)
+        return nothing
+
+    lax.fori_loop(0, AZ, body, 0, unroll=8)
 
 
 def kernel(
-    state, counts, speeds, spins, out,
-    packed, wide, moved, evolved, *scratch,
+    state_hbm, counts_hbm, speeds_hbm, out,
+    state, counts, speeds, packed, wide, evolved, *scratch,
 ):
     received = scratch[0:4]
     carried = scratch[4:8]
@@ -127,7 +131,14 @@
     cell_above = scratch[16:20]
     row_south, row_north = scratch[20:22]
     (in_send, in_recv, out_send, out_recv, own, up_send, up_recv, down_send, down_recv,
-     row_send, row_recv, edge_send, edge_recv) = scratch[22:]
+     row_send, row_recv, edge_send, edge_recv, load) = scratch[22:]
+
+    loads = [
+        pltpu.make_async_copy(source, target, load.at[i])
+        for i, (source, target) in enumerate(
+            [(state_hbm, state), (counts_hbm, counts), (speeds_hbm, speeds)]
+        )
+    ]
 
     me = lax.axis_index("az")
     rad = lax.axis_index("rad")
@@ -147,13 +158,21 @@
     for other in (rad_next, rad_last):
         pl.semaphore_signal(barrier, inc=1, device_id={"rad": other}, device_id_type=MESH)
 
-    def pack(row, carry):
-        for cell in range(NZ):
-            packed[row, cell] = state[pl.ds(cell * ROWS + row, FIELDS, stride=NZ * ROWS), :]
-        return carry
-
-    lax.fori_loop(0, ROWS, pack, 0)
-    pl.semaphore_wait(barrier, AZ + 1)
+    for copy in loads:
+        copy.start()
+    tables = field_tables()
+
+    def pack(c):
+        def body(i, carry):
+            row = PART * i + c
+            for cell in range(NZ):
+                packed[row, cell] = state[pl.ds(cell * ROWS + row, FIELDS, stride=NZ * ROWS), :]
+            return carry
+
+        lax.fori_loop(0, ROWS // PART, body, 0)
+
+    def partner(k):
+        return lax.rem(me + AZ + (k + 1) // 2 * (2 * lax.rem(k, 2) - 1), AZ)
 
     def send_in(c):
         own_copy = pltpu.make_async_copy(
@@ -162,7 +181,7 @@
         own_copy.start()
 
         def body(k, carry):
-            to = lax.rem(me + k, AZ)
+            to = partner(k)
             to_block, to_quarter = place(to, rad)
             pltpu.make_async_remote_copy(
                 src_ref=packed.at[PART * to_block + c, pl.ds(PART * to_quarter, PART)],
@@ -185,7 +204,7 @@
         own_copy.start()
 
         def body(k, carry):
-            to = lax.rem(me + k, AZ)
+            to = partner(k)
             pltpu.make_async_remote_copy(
                 src_ref=ready[c].at[to],
                 dst_ref=wide.at[1 + PART * block + c, pl.ds(PART * quarter, PART)],
@@ -238,17 +257,16 @@
 
     def first_step(c):
         row = PART * block + c
-        transport(received[c], moved, speeds[row])
-        rotate(moved, carried[c], counts[row])
+        carry(received[c], carried[c], speeds[row], counts[row])
 
     has_south = jnp.logical_or(rad > 0, block > 0)
     has_north = jnp.logical_or(rad < RAD - 1, block < Z_CHIPS - 1)
 
     def second_step(c):
         row = PART * block + c
-        spin = spins[row]
-
-        def body(k, carry):
+        spin = spin_of(row, rad, tables[-1])
+
+        def body(k, nothing):
             v = carried[c][k]
             if c > 0:
                 south = carried[c - 1][k]
@@ -262,12 +280,11 @@
                 north = jnp.where(has_north, north, jnp.zeros_like(north))
             up = jnp.concatenate([v[1:], cell_above[c][k][None]], axis=0)
             down = jnp.concatenate([cell_below[c][k][None], v[:-1]], axis=0)
-            evolved[k] = evolve(v, north, south, up, down, spin)
-            return carry
-
-        lax.fori_loop(0, AZ, body, 0)
-        transport(evolved, moved, speeds[row])
-        rotate(moved, ready[c], counts[row])
+            evolved[k] = evolve(v, north, south, up, down, tables, spin)
+            return nothing
+
+        lax.fori_loop(0, AZ, body, 0, unroll=4)
+        carry(evolved, ready[c], speeds[row], counts[row])
 
     ins, outs, halos = {}, {}, {}
 
@@ -283,8 +300,16 @@
         outs[c].wait()
         whole(ready[c], out_send.at[c], out_recv.at[c]).wait_recv()
 
+    loads[0].wait()
+    pack(0)
+    pl.semaphore_wait(barrier, AZ + 1)
     ins[0] = send_in(0)
+    pack(3)
     ins[3] = send_in(3)
+    pack(1)
+    pack(2)
+    loads[1].wait()
+    loads[2].wait()
 
     wait_in(0)
     ins[1] = send_in(1)
@@ -333,8 +358,6 @@
     edge_last = edge(0, 1, ROWS + 1, rad_last)
     wait_out(3)
     edge_next = edge(1, ROWS, 0, rad_next)
-    wait_out(1)
-    wait_out(2)
     edge_last.wait()
     edge_next.wait()
 
@@ -346,18 +369,29 @@
     def _():
         wide[ROWS + 1] = jnp.zeros((NZ, FIELDS, LANES), jnp.float32)
 
-    def last(row, carry):
-        spin = spins[row]
+    def last(row):
+        spin = spin_of(row, rad, tables[-1])
         for cell in range(NZ):
             pick = lambda r, c: wide[r, c][None]
             result = evolve(
                 pick(row + 1, cell), pick(row + 2, cell), pick(row, cell),
-                pick(row + 1, (cell + 1) % NZ), pick(row + 1, (cell + NZ - 1) % NZ), spin,
+                pick(row + 1, (cell + 1) % NZ), pick(row + 1, (cell + NZ - 1) % NZ), tables, spin,
             )
             out[pl.ds(cell * ROWS + row, FIELDS, stride=NZ * ROWS), :] = result[0]
-        return carry
-
-    lax.fori_loop(0, ROWS, last, 0)
+
+    def last_first(i, nothing):
+        last(PART * i)
+        return nothing
+
+    def last_others(i, nothing):
+        for c in range(1, PART):
+            last(PART * i + c)
+        return nothing
+
+    wait_out(1)
+    lax.fori_loop(0, ROWS // PART, last_first, 0)
+    wait_out(2)
+    lax.fori_loop(0, ROWS // PART, last_others, 0)
 
     for c in ORDER:
         whole(received[c], in_send.at[c], in_recv.at[c]).wait_send()
@@ -369,22 +403,22 @@
 
 
 def shards(state, shift_counts, residual_speed):
-    radius = (lax.axis_index("rad") * ROWS + jnp.arange(ROWS, dtype=jnp.int32)).astype(jnp.float32)
-    omega = (1.0 + radius / (ROWS * RAD)) ** (-1.5)
     circle = (AZ, PART, FIELDS, LANES)
     vmem = pl.BlockSpec(memory_space=pltpu.VMEM)
-    smem = pl.BlockSpec(memory_space=pltpu.SMEM)
+    hbm = pl.BlockSpec(memory_space=pltpu.HBM)
     f32 = jnp.float32
     dma = pltpu.SemaphoreType.DMA
     result = pl.pallas_call(
         kernel,
         out_shape=jax.ShapeDtypeStruct((FIELDS * NZ * ROWS, LANES), f32),
-        in_specs=[vmem, smem, smem, smem],
+        in_specs=[hbm, hbm, hbm],
         out_specs=vmem,
         scratch_shapes=[
+            pltpu.VMEM((FIELDS * NZ * ROWS, LANES), f32),
+            pltpu.SMEM((ROWS,), jnp.int32),
+            pltpu.SMEM((ROWS,), f32),
             pltpu.VMEM((ROWS, NZ, FIELDS, LANES), f32),
             pltpu.VMEM((ROWS + 2, NZ, FIELDS, LANES), f32),
-            pltpu.VMEM(circle, f32),
             pltpu.VMEM(circle, f32),
         ]
         + [pltpu.VMEM(circle, f32)] * 12
@@ -392,11 +426,11 @@
         + [pltpu.VMEM(circle, f32)] * 2
         + [dma((4,)), dma((4,)), dma((4,)), dma((4,)), dma((8,))]
         + [dma((4,)), dma((4,)), dma((4,)), dma((4,))]
-        + [dma((2,)), dma((2,)), dma((2,)), dma((2,))],
+        + [dma((2,)), dma((2,)), dma((2,)), dma((2,)), dma((3,))],
         compiler_params=pltpu.CompilerParams(
             collective_id=0, has_side_effects=True, vmem_limit_bytes=48 << 20
         ),
-    )(state.reshape(FIELDS * NZ * ROWS, LANES), shift_counts, residual_speed, omega)
+    )(state.reshape(FIELDS * NZ * ROWS, LANES), shift_counts, residual_speed)
     return result.reshape(FIELDS, NZ, ROWS, LANES)
 
 

time: 128 us -> 123 us (0.961)
  Pallas kernels: 123 us -> 119 us
    pallas_call x1, Pallas kernels: 123 us -> 119 us  [shards(): pl.pallas_call(kernel, out_shape=jax.ShapeDtypeStruct((FIELDS * NZ * ROWS...]
where the time goes in v2:
time: 123 us
  Pallas kernels  119 us (97%)
  local copies, waits for them, and re-layouts  4.22 us (3%)
    pallas_call x1, Pallas kernels, shards(): pl.pallas_call(kernel, out_shape=jax.ShapeDtypeStruct((FIELDS * NZ * ROWS...  119 us
    unnamed x7, local copies, waits for them, and re-layouts  4.22 us

profile of v2, /device:TPU:1, one launch (start us, length us, event | category | flops | bytes accessed | tf_op | source)
XLA Modules:
  0.0 123.1 jit_solution(17309022384093124873)
XLA Ops:
  0.0 0.0 copy-start
  0.0 1.6 %copy-done = f32[8,16,32,128]{3,2,1,0:T(8,128)S(1)} copy-done((f32[8,16,32,128]{3,2,1,0:T(8,128)S(1)}, f32[8,16,32,128]{3,2,1,0:T(8,128)}, u32[]{:S(2)}) %copy-start) | copy-done | bytes 2097176
  1.6 0.0 copy-start.1
  1.6 0.7 copy-done.1
  2.2 0.0 copy-start.2
  2.2 0.7 copy-done.2
  2.9 118.8 %shard_map.37 = f32[4096,128]{1,0:T(8,128)S(1)} custom-call(f32[4096,128]{1,0:T(8,128)S(1)} %bitcast.3, s32[32]{0:T(128)S(1)} %copy-done.1, f32[32]{0:T(128)S(1)} %copy-done.2), custom_call_target="tpu_custom_call" | custom-call | tf_op jit(solution)/shard_map/pallas_call | solution.py:411
  121.8 1.3 %copy.5 = f32[8,16,32,128]{3,2,1,0:T(8,128)} copy(f32[8,16,32,128]{3,2,1,0:T(8,128)S(1)} %bitcast.2) | data formatting | bytes 4194304
Async XLA Ops:
  0.0 1.6 %copy-start = (f32[8,16,32,128]{3,2,1,0:T(8,128)S(1)}, f32[8,16,32,128]{3,2,1,0:T(8,128)}, u32[]{:S(2)}) copy-start(f32[8,16,32,128]{3,2,1,0:T(8,128)} %param.3) | copy-start | bytes 6291460
  1.6 0.7 copy-start.1
  2.2 0.7 copy-start.2

commit v3 on v2

--- a/solution.py
+++ b/solution.py
@@ -10,6 +10,10 @@
 Z_CHIPS = 8
 PART = 4
 ORDER = (0, 3, 1, 2)
+TILES = AZ * PART
+BORDER = 7 * TILES
+LAST = 2
+LAST_PARTS = ((0, 1), (2, 3))
 
 time_step = 0.2
 viscosity = 0.1
@@ -73,7 +77,26 @@
                 0.0,
             ]
         ),
+        field_vector([0, 7, 2, 3, 4, 5, 6, 2]),
+        field_vector([1, 1, 2, 3, 4, 5, 1, 2]),
+        field_vector([1.0, 1.0, 0.0, 0.0, 0.0, 0.0, 1.0, 0.0]),
+        field_vector([0, 0, 2, 3, 4, 5, 6, 1]),
+        field_vector([1.0, -1.0, 1.0, 1.0, 1.0, 1.0, 1.0, 1.0]),
     )
+
+
+def gathered(value, source):
+    return picked(value[None], source)[0]
+
+
+def bordering(value, tables, sign):
+    first, second, factor = tables[6:9]
+    return gathered(value, first) - (sign * factor) * gathered(value, second)
+
+
+def border_terms(value, tables, north):
+    term = viscosity * gathered(value, tables[9])
+    return tables[10] * term if north else term
 
 
 def spin_of(row, rad, spin_factor):
@@ -83,7 +106,7 @@
 
 
 def evolve(v, north, south, up, down, tables, spin):
-    from_radial, from_vertical, from_spin, radial_factor, vertical_factor, _ = tables
+    from_radial, from_vertical, from_spin, radial_factor, vertical_factor = tables[:5]
     laplacian = (north + south) + (up + down) - 4.0 * v
     rates = (
         radial_factor * picked(north - south, from_radial)
@@ -129,9 +152,9 @@
     ready = scratch[8:12]
     cell_below = scratch[12:16]
     cell_above = scratch[16:20]
-    row_south, row_north = scratch[20:22]
+    row_south, row_north, border_last, border_next = scratch[20:24]
     (in_send, in_recv, out_send, out_recv, own, up_send, up_recv, down_send, down_recv,
-     row_send, row_recv, edge_send, edge_recv, load) = scratch[22:]
+     row_send, row_recv, edge_send, edge_recv, load) = scratch[24:]
 
     loads = [
         pltpu.make_async_copy(source, target, load.at[i])
@@ -161,6 +184,8 @@
     for copy in loads:
         copy.start()
     tables = field_tables()
+    for border in (row_south, row_north):
+        border[pl.ds(BORDER, TILES), :] = jnp.zeros((TILES, LANES), jnp.float32)
 
     def pack(c):
         def body(i, carry):
@@ -196,27 +221,34 @@
         lax.fori_loop(1, AZ, body, 0)
         return own_copy
 
-    def send_out(c):
+    def send_out(c, part=0, cells=(0, 1, 2, 3)):
+        first, count = cells[0], len(cells)
+        target = wide.at[1 + PART * block + c, pl.ds(PART * quarter + first, count)]
         own_copy = pltpu.make_async_copy(
-            ready[c].at[me], wide.at[1 + PART * block + c, pl.ds(PART * quarter, PART)],
-            own.at[PART + c],
+            ready[c].at[me, pl.ds(first, count)], target, own.at[PART + c if part == 0 else 2 * PART - 1 + part]
         )
         own_copy.start()
+        which = c if part == 0 else PART - 1 + part
 
         def body(k, carry):
             to = partner(k)
             pltpu.make_async_remote_copy(
-                src_ref=ready[c].at[to],
-                dst_ref=wide.at[1 + PART * block + c, pl.ds(PART * quarter, PART)],
-                send_sem=out_send.at[c],
-                recv_sem=out_recv.at[c],
+                src_ref=ready[c].at[to, pl.ds(first, count)],
+                dst_ref=target,
+                send_sem=out_send.at[which],
+                recv_sem=out_recv.at[which],
                 device_id={"az": to},
                 device_id_type=MESH,
             ).start()
             return carry
 
         lax.fori_loop(1, AZ, body, 0)
-        return own_copy
+        part_of = ready[c].at[pl.ds(0, AZ - 1), pl.ds(first, count)]
+        return own_copy, pltpu.make_async_remote_copy(
+            src_ref=part_of, dst_ref=part_of,
+            send_sem=out_send.at[which], recv_sem=out_recv.at[which],
+            device_id={"az": lax.rem(me + 1, AZ)}, device_id_type=MESH,
+        )
 
     def whole(buffer, send_sem, recv_sem):
         part = buffer.at[pl.ds(0, AZ - 1)]
@@ -242,12 +274,22 @@
         up.start()
         return down, up
 
-    def row_copy(which, source, target, step):
+    def row_copy(which, row, packing, target, sign):
+        def body(k, nothing):
+            value = row[k]
+            for cell in range(PART):
+                packing[pl.ds(k * PART + cell, FIELDS, stride=TILES), :] = bordering(
+                    value[cell], tables, sign
+                )
+            return nothing
+
+        lax.fori_loop(0, AZ, body, 0, unroll=2)
+        step = -sign
         other = block + step
         to_rad = lax.rem(rad + (other + Z_CHIPS) // Z_CHIPS - 1 + RAD, RAD)
         to_block = lax.rem(other + Z_CHIPS, Z_CHIPS)
         copy = pltpu.make_async_remote_copy(
-            src_ref=source, dst_ref=target,
+            src_ref=packing.at[pl.ds(0, BORDER)], dst_ref=target.at[pl.ds(0, BORDER)],
             send_sem=row_send.at[which], recv_sem=row_recv.at[which],
             device_id={"az": owner(to_block, quarter, to_rad), "rad": to_rad},
             device_id_type=MESH,
@@ -264,23 +306,27 @@
 
     def second_step(c):
         row = PART * block + c
-        spin = spin_of(row, rad, tables[-1])
+        spin = spin_of(row, rad, tables[5])
 
         def body(k, nothing):
             v = carried[c][k]
-            if c > 0:
-                south = carried[c - 1][k]
-            else:
-                south = row_south[k]
-                south = jnp.where(has_south, south, jnp.zeros_like(south))
-            if c < PART - 1:
-                north = carried[c + 1][k]
-            else:
-                north = row_north[k]
-                north = jnp.where(has_north, north, jnp.zeros_like(north))
+            south = carried[c - 1][k] if c > 0 else jnp.zeros_like(v)
+            north = carried[c + 1][k] if c < PART - 1 else jnp.zeros_like(v)
             up = jnp.concatenate([v[1:], cell_above[c][k][None]], axis=0)
             down = jnp.concatenate([cell_below[c][k][None], v[:-1]], axis=0)
-            evolved[k] = evolve(v, north, south, up, down, tables, spin)
+            result = evolve(v, north, south, up, down, tables, spin)
+            if c in (0, PART - 1):
+                border, inside = (row_south, has_south) if c == 0 else (row_north, has_north)
+                terms = jnp.stack(
+                    [
+                        border_terms(
+                            border[pl.ds(k * PART + cell, FIELDS, stride=TILES), :], tables, c > 0
+                        )
+                        for cell in range(PART)
+                    ]
+                )
+                result = result + jnp.where(inside, terms, jnp.zeros_like(terms))
+            evolved[k] = result
             return nothing
 
         lax.fori_loop(0, AZ, body, 0, unroll=4)
@@ -297,8 +343,8 @@
             copy.wait_recv()
 
     def wait_out(c):
-        outs[c].wait()
-        whole(ready[c], out_send.at[c], out_recv.at[c]).wait_recv()
+        outs[c][0].wait()
+        outs[c][1].wait_recv()
 
     loads[0].wait()
     pack(0)
@@ -314,13 +360,13 @@
     wait_in(0)
     ins[1] = send_in(1)
     first_step(0)
-    to_last = row_copy(0, carried[0], row_north, -1)
+    to_last = row_copy(0, carried[0], border_last, row_north, 1)
     halos[0] = cells(0)
 
     wait_in(3)
     ins[2] = send_in(2)
     first_step(3)
-    to_next = row_copy(1, carried[3], row_south, 1)
+    to_next = row_copy(1, carried[3], border_next, row_south, -1)
     halos[3] = cells(3)
 
     wait_in(1)
@@ -340,10 +386,13 @@
     wait_cells(3)
     second_step(3)
     outs[3] = send_out(3)
-    for c in (1, 2):
-        wait_cells(c)
-        second_step(c)
-        outs[c] = send_out(c)
+    wait_cells(1)
+    second_step(1)
+    outs[1] = send_out(1)
+    wait_cells(LAST)
+    second_step(LAST)
+    for part, cells_of_part in enumerate(LAST_PARTS):
+        outs["last", part] = send_out(LAST, part, cells_of_part)
 
     def edge(which, source, target, to):
         copy = pltpu.make_async_remote_copy(
@@ -369,9 +418,9 @@
     def _():
         wide[ROWS + 1] = jnp.zeros((NZ, FIELDS, LANES), jnp.float32)
 
-    def last(row):
-        spin = spin_of(row, rad, tables[-1])
-        for cell in range(NZ):
+    def last(row, cells):
+        spin = spin_of(row, rad, tables[5])
+        for cell in cells:
             pick = lambda r, c: wide[r, c][None]
             result = evolve(
                 pick(row + 1, cell), pick(row + 2, cell), pick(row, cell),
@@ -379,25 +428,30 @@
             )
             out[pl.ds(cell * ROWS + row, FIELDS, stride=NZ * ROWS), :] = result[0]
 
-    def last_first(i, nothing):
-        last(PART * i)
-        return nothing
-
-    def last_others(i, nothing):
-        for c in range(1, PART):
-            last(PART * i + c)
-        return nothing
+    def last_rows(work):
+        def body(i, nothing):
+            for c, cells in work:
+                last(PART * i + c, [cell for cell in range(NZ) if cell % PART in cells])
+            return nothing
+
+        lax.fori_loop(0, ROWS // PART, body, 0)
 
     wait_out(1)
-    lax.fori_loop(0, ROWS // PART, last_first, 0)
-    wait_out(2)
-    lax.fori_loop(0, ROWS // PART, last_others, 0)
+    last_rows([(0, range(PART))])
+    arrived, done = set(), set()
+    for part, cells_of_part in enumerate(LAST_PARTS):
+        wait_out(("last", part))
+        arrived |= set(cells_of_part)
+        inner = {j for j in arrived if {(j + 1) % PART, (j + PART - 1) % PART} <= arrived}
+        last_rows([(1, set(cells_of_part)), (3, set(cells_of_part)), (LAST, inner - done)])
+        done |= inner
 
     for c in ORDER:
         whole(received[c], in_send.at[c], in_recv.at[c]).wait_send()
-        whole(ready[c], out_send.at[c], out_recv.at[c]).wait_send()
         for copy in halos[c]:
             copy.wait_send()
+    for _, copy in outs.values():
+        copy.wait_send()
     to_last.wait_send()
     to_next.wait_send()
 
@@ -423,12 +477,12 @@
         ]
         + [pltpu.VMEM(circle, f32)] * 12
         + [pltpu.VMEM((AZ, FIELDS, LANES), f32)] * 8
-        + [pltpu.VMEM(circle, f32)] * 2
-        + [dma((4,)), dma((4,)), dma((4,)), dma((4,)), dma((8,))]
+        + [pltpu.VMEM((FIELDS * TILES, LANES), f32)] * 4
+        + [dma((4,)), dma((4,)), dma((8,)), dma((8,)), dma((12,))]
         + [dma((4,)), dma((4,)), dma((4,)), dma((4,))]
         + [dma((2,)), dma((2,)), dma((2,)), dma((2,)), dma((3,))],
         compiler_params=pltpu.CompilerParams(
-            collective_id=0, has_side_effects=True, vmem_limit_bytes=48 << 20
+            collective_id=0, has_side_effects=True, vmem_limit_bytes=50 << 20
         ),
     )(state.reshape(FIELDS * NZ * ROWS, LANES), shift_counts, residual_speed)
     return result.reshape(FIELDS, NZ, ROWS, LANES)

time: 123 us -> 120 us (0.976)
  Pallas kernels: 119 us -> 117 us
  local copies, waits for them, and re-layouts: 4.22 us -> 2.63 us
    pallas_call x1, Pallas kernels: 119 us -> 117 us  [shards(): pl.pallas_call(kernel, out_shape=jax.ShapeDtypeStruct((FIELDS * NZ * ROWS...]
    unnamed x7 -> x5, local copies, waits for them, and re-layouts: 4.22 us -> 2.63 us
where the time goes in v3:
time: 120 us
  Pallas kernels  117 us (98%)
  local copies, waits for them, and re-layouts  2.63 us (2%)
    pallas_call x1, Pallas kernels, shards(): pl.pallas_call(kernel, out_shape=jax.ShapeDtypeStruct((FIELDS * NZ * ROWS...  117 us
    unnamed x5, local copies, waits for them, and re-layouts  2.63 us

profile of v3, /device:TPU:1, one launch (start us, length us, event | category | flops | bytes accessed | tf_op | source)
XLA Modules:
  0.0 119.9 jit_solution(11911868853002832826)
XLA Ops:
  0.0 0.0 copy-start
  0.0 0.7 copy-done
  0.7 0.0 copy-start.1
  0.7 0.7 copy-done.1
  1.3 117.2 %shard_map.37 = f32[4096,128]{1,0:T(8,128)S(1)} custom-call(f32[4096,128]{1,0:T(8,128)} %bitcast.3, s32[32]{0:T(128)S(1)} %copy-done, f32[32]{0:T(128)S(1)} %copy-done.1), custom_call_target="tpu_custom_call" | custom-call | tf_op jit(solution)/shard_map/pallas_call | solution.py:465
  118.6 1.3 %copy.5 = f32[8,16,32,128]{3,2,1,0:T(8,128)} copy(f32[8,16,32,128]{3,2,1,0:T(8,128)S(1)} %bitcast.2) | data formatting | bytes 4194304
Async XLA Ops:
  0.0 0.7 copy-start
  0.7 0.7 copy-start.1

commit v4 on v3

--- a/solution.py
+++ b/solution.py
@@ -13,7 +13,7 @@
 TILES = AZ * PART
 BORDER = 7 * TILES
 LAST = 2
-LAST_PARTS = ((0, 1), (2, 3))
+LAST_PARTS = ((0, 1), (2,), (3,))
 
 time_step = 0.2
 viscosity = 0.1
@@ -169,6 +169,8 @@
     rad_last = lax.rem(rad + RAD - 1, RAD)
     block, quarter = place(me, rad)
 
+    for copy in loads:
+        copy.start()
     barrier = pltpu.get_barrier_semaphore()
 
     def greet(k, carry):
@@ -181,8 +183,6 @@
     for other in (rad_next, rad_last):
         pl.semaphore_signal(barrier, inc=1, device_id={"rad": other}, device_id_type=MESH)
 
-    for copy in loads:
-        copy.start()
     tables = field_tables()
     for border in (row_south, row_north):
         border[pl.ds(BORDER, TILES), :] = jnp.zeros((TILES, LANES), jnp.float32)
@@ -364,12 +364,12 @@
     halos[0] = cells(0)
 
     wait_in(3)
-    ins[2] = send_in(2)
     first_step(3)
     to_next = row_copy(1, carried[3], border_next, row_south, -1)
     halos[3] = cells(3)
 
     wait_in(1)
+    ins[2] = send_in(2)
     first_step(1)
     halos[1] = cells(1)
 

time: 120 us -> 118 us (0.983)
  Pallas kernels: 117 us -> 115 us
    pallas_call x1, Pallas kernels: 117 us -> 115 us  [shards(): pl.pallas_call(kernel, out_shape=jax.ShapeDtypeStruct((FIELDS * NZ * ROWS...]
where the time goes in v4:
time: 118 us
  Pallas kernels  115 us (97%)
  local copies, waits for them, and re-layouts  2.63 us (2%)
    pallas_call x1, Pallas kernels, shards(): pl.pallas_call(kernel, out_shape=jax.ShapeDtypeStruct((FIELDS * NZ * ROWS...  115 us
    unnamed x5, local copies, waits for them, and re-layouts  2.63 us

profile of v4, /device:TPU:1, one launch (start us, length us, event | category | flops | bytes accessed | tf_op | source)
XLA Modules:
  0.0 117.7 jit_solution(15547590733570345167)
XLA Ops:
  0.0 0.0 copy-start
  0.0 0.7 copy-done
  0.7 0.0 copy-start.1
  0.7 0.7 copy-done.1
  1.3 115.1 %shard_map.37 = f32[4096,128]{1,0:T(8,128)S(1)} custom-call(f32[4096,128]{1,0:T(8,128)} %bitcast.3, s32[32]{0:T(128)S(1)} %copy-done, f32[32]{0:T(128)S(1)} %copy-done.1), custom_call_target="tpu_custom_call" | custom-call | tf_op jit(solution)/shard_map/pallas_call | solution.py:465
  116.4 1.3 %copy.5 = f32[8,16,32,128]{3,2,1,0:T(8,128)} copy(f32[8,16,32,128]{3,2,1,0:T(8,128)S(1)} %bitcast.2) | data formatting | bytes 4194304
Async XLA Ops:
  0.0 0.7 copy-start
  0.7 0.7 copy-start.1

commit v5 on v4

--- a/solution.py
+++ b/solution.py
@@ -221,22 +221,21 @@
         lax.fori_loop(1, AZ, body, 0)
         return own_copy
 
-    def send_out(c, part=0, cells=(0, 1, 2, 3)):
+    def send_out(c, slot, cells=(0, 1, 2, 3)):
         first, count = cells[0], len(cells)
         target = wide.at[1 + PART * block + c, pl.ds(PART * quarter + first, count)]
         own_copy = pltpu.make_async_copy(
-            ready[c].at[me, pl.ds(first, count)], target, own.at[PART + c if part == 0 else 2 * PART - 1 + part]
+            ready[c].at[me, pl.ds(first, count)], target, own.at[PART + slot]
         )
         own_copy.start()
-        which = c if part == 0 else PART - 1 + part
 
         def body(k, carry):
             to = partner(k)
             pltpu.make_async_remote_copy(
                 src_ref=ready[c].at[to, pl.ds(first, count)],
                 dst_ref=target,
-                send_sem=out_send.at[which],
-                recv_sem=out_recv.at[which],
+                send_sem=out_send.at[slot],
+                recv_sem=out_recv.at[slot],
                 device_id={"az": to},
                 device_id_type=MESH,
             ).start()
@@ -246,7 +245,7 @@
         part_of = ready[c].at[pl.ds(0, AZ - 1), pl.ds(first, count)]
         return own_copy, pltpu.make_async_remote_copy(
             src_ref=part_of, dst_ref=part_of,
-            send_sem=out_send.at[which], recv_sem=out_recv.at[which],
+            send_sem=out_send.at[slot], recv_sem=out_recv.at[slot],
             device_id={"az": lax.rem(me + 1, AZ)}, device_id_type=MESH,
         )
 
@@ -351,9 +350,9 @@
     pl.semaphore_wait(barrier, AZ + 1)
     ins[0] = send_in(0)
     pack(3)
-    ins[3] = send_in(3)
     pack(1)
     pack(2)
+    ins[3] = send_in(3)
     loads[1].wait()
     loads[2].wait()
 
@@ -376,23 +375,24 @@
     to_next.wait_recv()
     wait_cells(0)
     second_step(0)
-    outs[0] = send_out(0)
+    outs[0] = send_out(0, 0, (0, 1))
 
     wait_in(2)
+    outs["rest"] = send_out(0, LAST, (2, 3))
     first_step(2)
     halos[2] = cells(2)
 
     to_last.wait_recv()
     wait_cells(3)
     second_step(3)
-    outs[3] = send_out(3)
+    outs[3] = send_out(3, 3)
     wait_cells(1)
     second_step(1)
-    outs[1] = send_out(1)
+    outs[1] = send_out(1, 1)
     wait_cells(LAST)
     second_step(LAST)
     for part, cells_of_part in enumerate(LAST_PARTS):
-        outs["last", part] = send_out(LAST, part, cells_of_part)
+        outs["last", part] = send_out(LAST, PART + part, cells_of_part)
 
     def edge(which, source, target, to):
         copy = pltpu.make_async_remote_copy(
@@ -404,6 +404,7 @@
         return copy
 
     wait_out(0)
+    wait_out("rest")
     edge_last = edge(0, 1, ROWS + 1, rad_last)
     wait_out(3)
     edge_next = edge(1, ROWS, 0, rad_next)

time: 118 us -> 117 us (level)
  no operation moved by 1% of the time
where the time goes in v5:
time: 117 us
  Pallas kernels  115 us (98%)
  local copies, waits for them, and re-layouts  2.63 us (2%)
    pallas_call x1, Pallas kernels, shards(): pl.pallas_call(kernel, out_shape=jax.ShapeDtypeStruct((FIELDS * NZ * ROWS...  115 us
    unnamed x5, local copies, waits for them, and re-layouts  2.63 us

profile of v5, /device:TPU:1, one launch (start us, length us, event | category | flops | bytes accessed | tf_op | source)
XLA Modules:
  0.0 117.3 jit_solution(13125497536570090613)
XLA Ops:
  0.0 0.0 copy-start
  0.0 0.7 copy-done
  0.7 0.0 copy-start.1
  0.7 0.7 copy-done.1
  1.3 114.7 %shard_map.37 = f32[4096,128]{1,0:T(8,128)S(1)} custom-call(f32[4096,128]{1,0:T(8,128)} %bitcast.3, s32[32]{0:T(128)S(1)} %copy-done, f32[32]{0:T(128)S(1)} %copy-done.1), custom_call_target="tpu_custom_call" | custom-call | tf_op jit(solution)/shard_map/pallas_call | solution.py:466
  116.0 1.3 %copy.5 = f32[8,16,32,128]{3,2,1,0:T(8,128)} copy(f32[8,16,32,128]{3,2,1,0:T(8,128)S(1)} %bitcast.2) | data formatting | bytes 4194304
Async XLA Ops:
  0.0 0.7 copy-start
  0.7 0.7 copy-start.1

commit v6 on v5

--- a/solution.py
+++ b/solution.py
@@ -13,7 +13,7 @@
 TILES = AZ * PART
 BORDER = 7 * TILES
 LAST = 2
-LAST_PARTS = ((0, 1), (2,), (3,))
+LAST_PARTS = ((0, 1, 2, 3),)
 
 time_step = 0.2
 viscosity = 0.1

time: 117 us -> 117 us (level)
  no operation moved by 1% of the time
where the time goes in v6:
time: 117 us
  Pallas kernels  114 us (97%)
  local copies, waits for them, and re-layouts  2.63 us (2%)
    pallas_call x1, Pallas kernels, shards(): pl.pallas_call(kernel, out_shape=jax.ShapeDtypeStruct((FIELDS * NZ * ROWS...  114 us
    unnamed x5, local copies, waits for them, and re-layouts  2.63 us

profile of v6, /device:TPU:1, one launch (start us, length us, event | category | flops | bytes accessed | tf_op | source)
XLA Modules:
  0.0 117.1 jit_solution(11882038331391014313)
XLA Ops:
  0.0 0.0 copy-start
  0.0 0.7 copy-done
  0.7 0.0 copy-start.1
  0.7 0.7 copy-done.1
  1.3 114.4 %shard_map.37 = f32[4096,128]{1,0:T(8,128)S(1)} custom-call(f32[4096,128]{1,0:T(8,128)} %bitcast.3, s32[32]{0:T(128)S(1)} %copy-done, f32[32]{0:T(128)S(1)} %copy-done.1), custom_call_target="tpu_custom_call" | custom-call | tf_op jit(solution)/shard_map/pallas_call | solution.py:466
  115.7 1.3 %copy.5 = f32[8,16,32,128]{3,2,1,0:T(8,128)} copy(f32[8,16,32,128]{3,2,1,0:T(8,128)S(1)} %bitcast.2) | data formatting | bytes 4194304
Async XLA Ops:
  0.0 0.7 copy-start
  0.7 0.7 copy-start.1

commit v7 on v6

--- a/solution.py
+++ b/solution.py
@@ -173,6 +173,9 @@
         copy.start()
     barrier = pltpu.get_barrier_semaphore()
 
+    for other in (rad_next, rad_last):
+        pl.semaphore_signal(barrier, inc=1, device_id={"rad": other}, device_id_type=MESH)
+
     def greet(k, carry):
         pl.semaphore_signal(
             barrier, inc=1, device_id={"az": lax.rem(me + k, AZ)}, device_id_type=MESH
@@ -180,8 +183,6 @@
         return carry
 
     lax.fori_loop(1, AZ, greet, 0)
-    for other in (rad_next, rad_last):
-        pl.semaphore_signal(barrier, inc=1, device_id={"rad": other}, device_id_type=MESH)
 
     tables = field_tables()
     for border in (row_south, row_north):
@@ -359,8 +360,8 @@
     wait_in(0)
     ins[1] = send_in(1)
     first_step(0)
+    halos[0] = cells(0)
     to_last = row_copy(0, carried[0], border_last, row_north, 1)
-    halos[0] = cells(0)
 
     wait_in(3)
     first_step(3)
@@ -370,13 +371,13 @@
     wait_in(1)
     ins[2] = send_in(2)
     first_step(1)
-    halos[1] = cells(1)
 
     to_next.wait_recv()
     wait_cells(0)
     second_step(0)
     outs[0] = send_out(0, 0, (0, 1))
 
+    halos[1] = cells(1)
     wait_in(2)
     outs["rest"] = send_out(0, LAST, (2, 3))
     first_step(2)

time: 117 us -> 117 us (level)
  no operation moved by 1% of the time
where the time goes in v7:
time: 117 us
  Pallas kernels  114 us (97%)
  local copies, waits for them, and re-layouts  2.63 us (2%)
    pallas_call x1, Pallas kernels, shards(): pl.pallas_call(kernel, out_shape=jax.ShapeDtypeStruct((FIELDS * NZ * ROWS...  114 us
    unnamed x5, local copies, waits for them, and re-layouts  2.63 us

profile of v7, /device:TPU:1, one launch (start us, length us, event | category | flops | bytes accessed | tf_op | source)
XLA Modules:
  0.0 116.5 jit_solution(15068558779231970433)
XLA Ops:
  0.0 0.0 copy-start
  0.0 0.7 copy-done
  0.7 0.0 copy-start.1
  0.7 0.7 copy-done.1
  1.3 113.9 %shard_map.37 = f32[4096,128]{1,0:T(8,128)S(1)} custom-call(f32[4096,128]{1,0:T(8,128)} %bitcast.3, s32[32]{0:T(128)S(1)} %copy-done, f32[32]{0:T(128)S(1)} %copy-done.1), custom_call_target="tpu_custom_call" | custom-call | tf_op jit(solution)/shard_map/pallas_call | solution.py:467
  115.2 1.3 %copy.5 = f32[8,16,32,128]{3,2,1,0:T(8,128)} copy(f32[8,16,32,128]{3,2,1,0:T(8,128)S(1)} %bitcast.2) | data formatting | bytes 4194304
Async XLA Ops:
  0.0 0.7 copy-start
  0.7 0.7 copy-start.1
